TPU v7x, 512 devices: a whole 4x4x16 slice. The times are simulated.
512 devices in a mesh: dp: 16 (over z), ep: 32 (over y, x, core).
Axes of the slice: x: 4, y: 4, z: 16, core: 2. Of those that a mesh axis runs over, the one named last changes fastest.
Arguments:
- upstream: bfloat16 [65536, 2880], P(('dp', 'ep')), may hold values from -6 to 6
- router_logits: float32 [65536, 4], P(('dp', 'ep')), may hold values from -4 to 4
- expert_ids: int32 [65536, 4], P(('dp', 'ep')), may hold values from 0 to 127, as said below
- guard_mask: int32 [65536], P(('dp', 'ep')), may hold values 0 or 1
- w_down: bfloat16 [11520, 2880], P('ep'), may hold values from -0.109375 to 0.109375
- saved_hidden: bfloat16 [11520, 16384], P('ep', 'dp'), may hold values from -0.59765625 to 0.59765625
Outputs:
- grad_hidden: bfloat16 [11520, 16384], P('ep', 'dp')
- grad_down: bfloat16 [2880, 11520], P('dp', 'ep')
- grad_logits: float32 [65536, 4], P(('dp', 'ep'))
Inputs may be any that keep to these rules, and one draw needn't show every extreme that they name: `expert_ids`: each row names 4 different experts. Among the rows of one device, each expert below 4 is named by at most 32 rows, and one of them by exactly 32 rows on every device.
All inputs are finite; a program needn't handle non-finite values. No bound on the sum of `guard_mask` on one device may be relied on, other than what follows from the above.
Results may differ from a plain program's by a relative error of at most 0.0057.
Values may be sent and summed in bfloat16 or wider, within the bound.
A program may use at most 128 MiB of HBM per device.

v0:
```python
import jax
import jax.numpy as jnp
from jax import lax
from jax.sharding import PartitionSpec as P

EXP_WIN = 4


def body(upstream, router_logits, expert_ids, guard_mask, w_down, saved_hidden):
    n_ep = lax.axis_size("ep")
    tok_rows = upstream.shape[0]
    width = upstream.shape[1]
    top_count = router_logits.shape[1]
    slot_count = saved_hidden.shape[1]
    capacity = slot_count // n_ep
    slices = n_ep // EXP_WIN
    probs = jax.nn.softmax(router_logits, axis=1)
    combine = probs.astype(jnp.bfloat16)
    live = (guard_mask[:, None] == 1) & (expert_ids < EXP_WIN)
    onehot = (
        (expert_ids[:, :, None] == jnp.arange(EXP_WIN, dtype=jnp.int32)[None, None, :])
        & live[:, :, None]
    ).astype(jnp.int32)
    flat = onehot.reshape(tok_rows * top_count, EXP_WIN)
    before = jnp.cumsum(flat, axis=0) - flat
    slot = jnp.sum(before * flat, axis=1)
    owner = jnp.sum(flat * jnp.arange(EXP_WIN, dtype=jnp.int32)[None, :], axis=1)
    target = jnp.where(jnp.sum(flat, axis=1) == 1, owner * capacity + slot, -1).reshape(
        tok_rows, top_count
    )
    picker = (
        target[:, :, None] == jnp.arange(EXP_WIN * capacity, dtype=jnp.int32)[None, None, :]
    ).astype(jnp.float32)
    select = jnp.sum(picker, axis=1).astype(jnp.bfloat16)
    send_rows = lax.dot_general(
        select, upstream, (((0,), (0,)), ((), ())), preferred_element_type=jnp.float32
    ).astype(jnp.bfloat16)
    send_weight = jnp.sum(picker * combine.astype(jnp.float32)[:, :, None], axis=(0, 1)).astype(
        jnp.bfloat16
    )
    send_rows = jnp.broadcast_to(
        send_rows.reshape(EXP_WIN, 1, capacity, width), (EXP_WIN, slices, capacity, width)
    ).reshape(n_ep, capacity, width)
    send_weight = jnp.broadcast_to(
        send_weight.reshape(EXP_WIN, 1, capacity), (EXP_WIN, slices, capacity)
    ).reshape(n_ep, capacity)
    recv_rows, recv_weight = (
        lax.all_to_all(send_rows, "ep", split_axis=0, concat_axis=0, tiled=True),
        lax.all_to_all(send_weight, "ep", split_axis=0, concat_axis=0, tiled=True),
    )
    recv_rows = recv_rows.reshape(slot_count, width)
    recv_weight = recv_weight.reshape(slot_count).astype(jnp.float32)
    image = lax.dot_general(
        w_down, recv_rows, (((1,), (1,)), ((), ())), preferred_element_type=jnp.float32
    )
    grad_hidden = (recv_weight[None, :] * image).astype(jnp.bfloat16)
    hidden_float = saved_hidden.astype(jnp.float32)
    partial_value = jnp.sum(hidden_float * image, axis=0)
    scaled = (recv_weight[None, :] * hidden_float).astype(jnp.bfloat16)
    returned = lax.all_to_all(
        partial_value.reshape(n_ep, capacity), "ep", split_axis=0, concat_axis=0, tiled=True
    )
    inner = jnp.sum(returned.reshape(EXP_WIN, slices, capacity), axis=1)
    dprob = jnp.sum(picker * inner.reshape(1, 1, EXP_WIN * capacity), axis=2)
    grad_logits = probs * (dprob - jnp.sum(probs * dprob, axis=1, keepdims=True))
    down_sum = lax.psum_scatter(
        lax.dot_general(
            recv_rows, scaled, (((0,), (1,)), ((), ())), preferred_element_type=jnp.float32
        ),
        "dp",
        scatter_dimension=0,
        tiled=True,
    )
    return (grad_hidden, down_sum.astype(jnp.bfloat16), grad_logits)


def solution(mesh):
    in_specs = (
        P(("dp", "ep"), None),
        P(("dp", "ep"), None),
        P(("dp", "ep"), None),
        P(("dp", "ep")),
        P("ep", None),
        P("ep", "dp"),
    )
    out_specs = (P("ep", "dp"), P("dp", "ep"), P(("dp", "ep"), None))
    return jax.shard_map(body, mesh=mesh, in_specs=in_specs, out_specs=out_specs, check_vma=False)
```

profile of v0, /device:TPU:1, one launch (start us, length us, event | category | flops | bytes accessed | tf_op | source)
XLA Modules:
  0.0 203.9 jit_solution(2683612434978075006)
XLA Ops:
  0.6 0.0 copy-start
  0.6 0.9 copy.37
  1.6 0.1 eq.65
  1.7 0.1 eq.57
  1.8 0.7 broadcast_compare_fusion
  2.5 0.7 compare_and_fusion
  3.2 0.1 copy.38
  3.3 0.1 and.32
  3.4 0.1 and.29
  3.5 1.2 reduce-window.6
  4.8 0.2 slice_reduce_fusion
  5.0 0.2 reduce-window.9
  5.2 0.1 add_bitcast_fusion
  5.3 0.1 select_n.12
  5.4 0.1 copy.41
  5.5 0.2 convert_reduce_fusion
  5.6 2.3 %convolution_convert_fusion = bf16[128,2880]{0,1:T(8,128)(2,1)} fusion(bf16[128,2880]{0,1:T(8,128)(2,1)} %param.6, bf16[128,128]{1,0:T(8,128)(2,1)S(1)} %convert_reduce_fusion), kind=kOutput, calls=%fused_computation | convolution fusion | flops 94740480 | bytes 1507328 | tf_op jit(solution)/shard_map/dot_general | solution.py:35
  7.9 1.5 copy.43
  9.4 3.0 %broadcast_in_dim.13 = bf16[4,8,32,2880]{3,2,1,0:T(8,128)(2,1)} broadcast(bf16[4,32,2880]{2,1,0:T(8,128)(2,1)S(1)} %bitcast.33), dimensions={0,2,3} | broadcast | bytes 6635520 | tf_op jit(solution)/shard_map/broadcast_in_dim | solution.py:41
  12.5 0.0 copy-start.1
  12.5 11.5 %all-to-all-start.1 = ((bf16[32,32,2880]{2,1,0:T(8,128)(2,1)}), bf16[32,32,2880]{2,1,0:T(8,128)(2,1)}, u32[]{:S(2)}, u32[]{:S(2)}) async-start(bf16[32,32,2880]{2,1,0:T(8,128)(2,1)} %bitcast.32), calls=%async_computation.1 | async-start | bytes 12058624 | tf_op jit(solution)/shard_map/all_to_all | solution.py:48
  23.9 0.0 copy-done.1
  24.0 69.9 %all-to-all-done.1 = bf16[32,32,2880]{2,1,0:T(8,128)(2,1)} async-done(((bf16[32,32,2880]{2,1,0:T(8,128)(2,1)}), bf16[32,32,2880]{2,1,0:T(8,128)(2,1)}, u32[]{:S(2)}, u32[]{:S(2)}) %all-to-all-start.1) | async-done | bytes 5898272 | tf_op jit(solution)/shard_map/all_to_all | solution.py:48
  93.9 0.0 copy-done
  93.9 6.5 %fusion.2 = (f32[1024]{0:T(1024)S(1)}, f32[1024,360]{0,1:T(8,128)}) fusion(bf16[360,1024]{1,0:T(8,128)(2,1)} %param.11, bf16[1024,2880]{1,0:T(8,128)(2,1)} %bitcast.4, bf16[360,2880]{1,0:T(8,128)(2,1)S(1)} %copy-done), kind=kOutput, calls=%fused_computation.4 | convolution fusion | flops 2124471296 | bytes 10187776 | tf_op jit(solution)/shard_map/dot_general | solution.py:53
  100.4 0.7 all_to_all.18
  101.1 8.6 %all-to-all-start.2 = ((f32[32,1,32]{2,1,0:T(1,128)}), f32[32,1,32]{2,1,0:T(1,128)S(1)}, u32[]{:S(2)}, u32[]{:S(2)}) async-start(f32[32,1,32]{2,1,0:T(1,128)} %all_to_all.18), calls=%async_computation.2 | async-start | bytes 32768 | tf_op jit(solution)/shard_map/all_to_all | solution.py:60
  109.7 1.3 dynamic-slice.4
  111.6 5.0 %all-to-all-done.2 = f32[32,1,32]{2,1,0:T(1,128)S(1)} async-done(((f32[32,1,32]{2,1,0:T(1,128)}), f32[32,1,32]{2,1,0:T(1,128)S(1)}, u32[]{:S(2)}, u32[]{:S(2)}) %all-to-all-start.2) | async-done | bytes 4128 | tf_op jit(solution)/shard_map/all_to_all | solution.py:60
  116.7 0.1 mul.74
  116.8 0.3 select_reduce_fusion
  117.1 0.1 convert_element_type.60
  117.2 0.6 copy.42
  117.8 4.1 %all-to-all-start = ((bf16[32,1,32]{2,1,0:T(2,128)(2,1)}), bf16[32,1,32]{2,1,0:T(2,128)(2,1)S(1)}, u32[]{:S(2)}, u32[]{:S(2)}) async-start(bf16[32,1,32]{2,1,0:T(2,128)(2,1)} %copy.42), calls=%async_computation | async-start | bytes 32768 | tf_op jit(solution)/shard_map/all_to_all | solution.py:49
  122.0 0.6 subtract_multiply_fusion
  122.5 6.4 %all-to-all-done = bf16[32,1,32]{2,1,0:T(2,128)(2,1)S(1)} async-done(((bf16[32,1,32]{2,1,0:T(2,128)(2,1)}), bf16[32,1,32]{2,1,0:T(2,128)(2,1)S(1)}, u32[]{:S(2)}, u32[]{:S(2)}) %all-to-all-start) | async-done | bytes 2080 | tf_op jit(solution)/shard_map/all_to_all | solution.py:49
  128.9 0.1 convert_reduce_fusion.1
  129.0 0.1 reshape.103
  129.1 8.3 %fusion.4 = f32[2880,360]{1,0:T(8,128)} fusion(bf16[1024,2880]{1,0:T(8,128)(2,1)} %bitcast.4, bf16[360,1024]{1,0:T(8,128)(2,1)} %param.11, f32[1024]{0:T(1024)S(1)} %reshape.103), kind=kOutput, calls=%fused_computation.7 | convolution fusion | flops 2124472320 | bytes 10786816 | tf_op jit(solution)/shard_map/dot_general | solution.py:67
  137.4 60.6 %fusion = f32[192,360]{1,0:T(8,128)S(1)} fusion(f32[2880,360]{1,0:T(8,128)} %fusion.4), kind=kCustom, calls=%all-reduce-scatter | all-reduce-scatter fusion | flops 1105921 | bytes 4425728
  198.0 2.1 %collective-permute-start = (bf16[180,360]{1,0:T(8,128)(2,1)S(1)}, bf16[180,360]{1,0:T(8,128)(2,1)S(1)}, u32[]{:S(2)}, u32[]{:S(2)}) collective-permute-start(bf16[180,360]{1,0:T(8,128)(2,1)S(1)} %slice.9), channel_id=1, source_target_pairs={{0,32},{32,64},{64,96},{96,128},{128,160},{160,192},{192,224},{224... | collective-permute-start | bytes 388808
  200.1 2.4 %fusion.3 = bf16[360,1024]{1,0:T(8,128)(2,1)} fusion(f32[1024,360]{0,1:T(8,128)} %get-tuple-element.9, f32[1024]{0:T(1024)S(1)} %reshape.103), kind=kLoop, calls=%fused_computation.6 | loop fusion | flops 737280 | bytes 2215936 | tf_op jit(solution)/shard_map/convert_element_type | solution.py:56
  202.5 0.0 collective-permute-done
  202.5 0.7 concatenate
  203.2 0.7 dynamic-slice_convert_fusion
  (10 shorter events, 0.2 us)
Async XLA Ops:
  0.6 93.3 %copy-start = (bf16[360,2880]{1,0:T(8,128)(2,1)S(1)}, bf16[360,2880]{1,0:T(8,128)(2,1)}, u32[]{:S(2)}) copy-start(bf16[360,2880]{1,0:T(8,128)(2,1)} %param.10) | copy-start | bytes 6220804
  12.5 11.5 %copy-start.1 = (f32[128,4]{0,1:T(4,128)S(1)}, f32[128,4]{0,1:T(4,128)}, u32[]{:S(2)}) copy-start(f32[128,4]{0,1:T(4,128)} %param.7) | copy-start | bytes 6148
  12.5 81.5 %all-to-all-start.1 = ((bf16[32,32,2880]{2,1,0:T(8,128)(2,1)}), bf16[32,32,2880]{2,1,0:T(8,128)(2,1)}, u32[]{:S(2)}, u32[]{:S(2)}) async-start(bf16[32,32,2880]{2,1,0:T(8,128)(2,1)} %bitcast.32), calls=%async_computation.1 | async-start | bytes 12058624 | tf_op jit(solution)/shard_map/all_to_all | solution.py:48
  101.1 15.5 %all-to-all-start.2 = ((f32[32,1,32]{2,1,0:T(1,128)}), f32[32,1,32]{2,1,0:T(1,128)S(1)}, u32[]{:S(2)}, u32[]{:S(2)}) async-start(f32[32,1,32]{2,1,0:T(1,128)} %all_to_all.18), calls=%async_computation.2 | async-start | bytes 32768 | tf_op jit(solution)/shard_map/all_to_all | solution.py:60
  117.8 11.1 %all-to-all-start = ((bf16[32,1,32]{2,1,0:T(2,128)(2,1)}), bf16[32,1,32]{2,1,0:T(2,128)(2,1)S(1)}, u32[]{:S(2)}, u32[]{:S(2)}) async-start(bf16[32,1,32]{2,1,0:T(2,128)(2,1)} %copy.42), calls=%async_computation | async-start | bytes 32768 | tf_op jit(solution)/shard_map/all_to_all | solution.py:49
  198.0 4.5 %collective-permute-start = (bf16[180,360]{1,0:T(8,128)(2,1)S(1)}, bf16[180,360]{1,0:T(8,128)(2,1)S(1)}, u32[]{:S(2)}, u32[]{:S(2)}) collective-permute-start(bf16[180,360]{1,0:T(8,128)(2,1)S(1)} %slice.9), channel_id=1, source_target_pairs={{0,32},{32,64},{64,96},{96,128},{128,160},{160,192},{192,224},{224... | collective-permute-start | bytes 388808
where the time goes:
time: 206 us; the launch traced here: 204 us
  waiting for transfers between devices  81.4 us (40%)
  blocking collectives  60.6 us (29%)
  starting transfers between devices  26.2 us (13%)
  matrix products  17.1 us (8%)
  local copies, waits for them, and re-layouts  10.7 us (5%)
  other arithmetic  6.48 us (3%)
    all_to_all x1, waiting for transfers between devices, body(): lax.all_to_all(send_rows, 'ep', split_axis=0, concat_axis=0, tiled=True)  69.9 us
    unnamed x1, blocking collectives  60.6 us
    all_to_all x1, starting transfers between devices, body(): lax.all_to_all(send_rows, 'ep', split_axis=0, concat_axis=0, tiled=True)  11.5 us
    all_to_all x1, starting transfers between devices, body(): lax.all_to_all(partial_value.reshape(n_ep, capacity), 'ep', split_axis=0,...  8.55 us
    dot_general x1, matrix products, body(): lax.dot_general(recv_rows, scaled, (((0,), (1,)), ((), ())), preferred_el...  8.31 us
    dot_general x1, matrix products, body(): lax.dot_general(w_down, recv_rows, (((1,), (1,)), ((), ())), preferred_el...  6.48 us
    all_to_all x1, waiting for transfers between devices, body(): lax.all_to_all(send_weight, 'ep', split_axis=0, concat_axis=0, tiled=True)  6.38 us
    all_to_all x1, waiting for transfers between devices, body(): lax.all_to_all(partial_value.reshape(n_ep, capacity), 'ep', split_axis=0,...  5.04 us
  transfers between devices with their start and end apart: 4, of which 3 were waited for; matrix products, arithmetic and copies ran while one was open for 2% of the time, Pallas kernels for 0%

commit v1 on v0

v1 whole, which is shorter than its diff:
```python
import functools

import jax
import jax.numpy as jnp
from jax import lax
from jax.experimental import pallas as pl
from jax.experimental.pallas import tpu as pltpu
from jax.sharding import PartitionSpec as P

MESH = pl.DeviceIdType.MESH
F32 = jnp.float32
BF16 = jnp.bfloat16

NE = 4
NX = 4
NJ = 8
NZ = 16
CAP = 32
TOK = 128
D = 2880
BLK = 180
PBLK = 192
NQ = 8
QW = 2 * PBLK
HID = 360
HPAD = 384
COLS = 1024
WLANE = BLK


def dot_nt(a, b):
    return lax.dot_general(a, b, (((1,), (1,)), ((), ())), preferred_element_type=F32)


def dot_nn(a, b):
    return lax.dot_general(a, b, (((1,), (0,)), ((), ())), preferred_element_type=F32)


def kernel(
    up_hbm, ids_ref, logits_ref, guard_ref, w_hbm, h_hbm,
    gh_hbm, gd_ref, gl_ref,
    up, upf, w, wq, h, scaled, rows, g, acc, gh, t_ref, sp, sm, rp, rm, sel, rs, rr, ri,
    in_sem, y_send, y_recv, x_send, xl_recv, xr_recv, xo_recv, s_send, s_recv,
    sp_send, rp_recv, sm_send, rm_recv, r1_send, r1_recv, r2_send, r2_recv, out_sem,
):
    z = lax.axis_index("dp")
    ep = lax.axis_index("ep")
    y = ep // NJ
    j = ep % NJ
    x = j // 2
    c = j % 2
    zr = lax.rem(z + 1, NZ)
    zl = lax.rem(z + NZ - 1, NZ)
    xr = lax.rem(x + 1, NX)
    xl = lax.rem(x + NX - 1, NX)
    xo = lax.rem(x + 2, NX)
    jr = xr * 2 + c
    jl = xl * 2 + c
    jo = xo * 2 + c
    js = x * 2 + (1 - c)
    half_z = z // 2

    cp_up = pltpu.make_async_copy(up_hbm, up, in_sem.at[0])
    cp_h = pltpu.make_async_copy(h_hbm, h, in_sem.at[1])
    cp_w = pltpu.make_async_copy(w_hbm, w, in_sem.at[2])
    cp_up.start()
    cp_h.start()
    cp_w.start()

    barrier = pltpu.get_barrier_semaphore()
    for d in range(1, NJ):
        pl.semaphore_signal(barrier, 1, device_id=(z, y * NJ + lax.rem(j + d, NJ)), device_id_type=MESH)
    for d in range(1, NE):
        pl.semaphore_signal(barrier, 1, device_id=(z, lax.rem(y + d, NE) * NJ + j), device_id_type=MESH)
    pl.semaphore_signal(barrier, 1, device_id=(zr, ep), device_id_type=MESH)
    pl.semaphore_signal(barrier, 1, device_id=(zl, ep), device_id_type=MESH)

    ids = ids_ref[...]
    logits = logits_ref[...]
    live = guard_ref[...] == 1
    top = jnp.max(logits, axis=0, keepdims=True)
    ex = jnp.exp(logits - top)
    probs = ex / jnp.sum(ex, axis=0, keepdims=True)
    combine = probs.astype(BF16).astype(F32)
    chosen = []
    weight = []
    for e in range(NE):
        hit = ((ids == e) & live).astype(F32)
        chosen.append(jnp.sum(hit, axis=0, keepdims=True))
        weight.append(jnp.sum(hit * combine, axis=0, keepdims=True))
    mask = jnp.concatenate(chosen + [jnp.zeros((8 - NE, TOK), F32)], axis=0)
    earlier = (
        lax.broadcasted_iota(jnp.int32, (TOK, TOK), 0) < lax.broadcasted_iota(jnp.int32, (TOK, TOK), 1)
    ).astype(F32).astype(BF16)
    slot = dot_nn(mask.astype(BF16), earlier)
    place = lax.broadcasted_iota(jnp.int32, (CAP, TOK), 0).astype(F32)
    picks = []
    wcols = []
    for e in range(NE):
        pick = jnp.where(slot[e:e + 1, :] == place, mask[e:e + 1, :], 0.0)
        picks.append(pick)
        wcols.append(jnp.sum(pick * weight[e], axis=1, keepdims=True))
    select = jnp.concatenate(picks, axis=0).astype(BF16)
    wcol = jnp.concatenate(wcols, axis=0)
    sel[...] = select
    at_weight = lax.broadcasted_iota(jnp.int32, (TOK, QW), 1) == WLANE

    cp_up.wait()
    upf[...] = up[...].astype(F32)
    gap = jnp.zeros((PBLK - BLK, TOK), F32)
    for q in range(NQ):
        a = q * 2 * BLK
        part = jnp.concatenate([upf[a:a + BLK, :], gap, upf[a + BLK:a + 2 * BLK, :], gap], axis=0)
        got = dot_nt(select, part.astype(BF16))
        rows[q] = jnp.where(at_weight, wcol, got).astype(BF16)

    def order(t):
        odd = lax.rem(t, 2)
        off = odd * ((t + 1) // 2) - (1 - odd) * (t // 2)
        return lax.rem(half_z + 4 + off + NQ, NQ)

    pl.semaphore_wait(barrier, NJ - 1 + NE - 1 + 2)

    def y_copy(t, d):
        q = order(t)
        e = lax.rem(y + d, NE)
        return pltpu.make_async_remote_copy(
            src_ref=rows.at[q, pl.ds(pl.multiple_of(e * CAP, CAP), CAP)],
            dst_ref=g.at[q, y, j],
            send_sem=y_send.at[t, d - 1],
            recv_sem=y_recv.at[t],
            device_id=(z, e * NJ + j),
            device_id_type=MESH,
        )

    def y_own(t):
        q = order(t)
        return pltpu.make_async_copy(
            rows.at[q, pl.ds(pl.multiple_of(y * CAP, CAP), CAP)], g.at[q, y, j], y_recv.at[t]
        )

    def x_copy(t, kind):
        q = order(t)
        src, to, sem = [
            (g.at[q, :, j], jr, xl_recv),
            (g.at[q, :, j], jl, xr_recv),
            (g.at[q, pl.ds(0, 2), jl], jr, xo_recv),
            (g.at[q, pl.ds(2, 2), jr], jl, xo_recv),
        ][kind]
        return pltpu.make_async_remote_copy(
            src_ref=src, dst_ref=src, send_sem=x_send.at[t, kind], recv_sem=sem.at[t],
            device_id=(z, y * NJ + to), device_id_type=MESH,
        )

    def s_copy(t, kind):
        q = order(t)
        piece = g.at[q, :, [j, jl, jr, jo][kind]]
        return pltpu.make_async_remote_copy(
            src_ref=piece, dst_ref=piece, send_sem=s_send.at[t, kind], recv_sem=s_recv.at[t],
            device_id=(z, y * NJ + js), device_id_type=MESH,
        )

    def wait_bytes(ref, sem):
        pltpu.make_async_copy(ref, ref, sem).wait()

    def start_y(t):
        y_own(t).start()
        for d in (2, 1, 3):
            y_copy(t, d).start()

    def own(t):
        wait_bytes(g.at[order(t), :, j], y_recv.at[t])
        x_copy(t, 0).start()
        x_copy(t, 1).start()
        s_copy(t, 0).start()

    def forward(t):
        q = order(t)
        wait_bytes(g.at[q, :, jl], xl_recv.at[t])
        x_copy(t, 2).start()
        s_copy(t, 1).start()
        wait_bytes(g.at[q, :, jr], xr_recv.at[t])
        x_copy(t, 3).start()
        s_copy(t, 2).start()

    def opposite(t):
        wait_bytes(g.at[order(t), :, jo], xo_recv.at[t])
        s_copy(t, 3).start()

    @pl.loop(0, NQ)
    def _(t):
        start_y(t)

    acc[...] = jnp.zeros_like(acc)
    cp_w.wait()
    wgap = jnp.zeros((HID, PBLK - BLK), BF16)
    for q in range(NQ):
        a = q * 2 * BLK
        wq[q] = jnp.concatenate([w[:, a:a + BLK], wgap, w[:, a + BLK:a + 2 * BLK], wgap], axis=1)

    own(0)
    own(1)
    forward(0)
    cp_h.wait()

    def plus_send(s):
        return pltpu.make_async_remote_copy(
            src_ref=sp.at[s], dst_ref=rp.at[s], send_sem=sp_send.at[s], recv_sem=rp_recv.at[s],
            device_id=(zr, ep), device_id_type=MESH,
        )

    def minus_send(s):
        return pltpu.make_async_remote_copy(
            src_ref=sm.at[s], dst_ref=rm.at[s], send_sem=sm_send.at[s], recv_sem=rm_recv.at[s],
            device_id=(zl, ep), device_id_type=MESH,
        )

    def plus(s):
        wait_bytes(rp.at[s - 1], rp_recv.at[s - 1])
        b = lax.rem(z + 8 - s + NZ, NZ)
        sp[s] = (t_ref[b] + rp[s - 1].astype(F32)).astype(BF16)
        plus_send(s).start()

    def minus(s):
        wait_bytes(rm.at[s - 1], rm_recv.at[s - 1])
        b = lax.rem(z + 9 + s, NZ)
        sm[s] = (t_ref[b] + rm[s - 1].astype(F32)).astype(BF16)
        minus_send(s).start()

    def column_weights(q):
        one = (lax.broadcasted_iota(jnp.int32, (8, 128), 1) == WLANE - 128).astype(F32).astype(BF16)
        tile = g[q, :, :, :, 128:256].reshape(COLS, 128)
        return dot_nt(one, tile)[0:1, :]

    @pl.loop(0, NQ)
    def _(t):
        q = order(t)

        @pl.when(t + 2 < NQ)
        def _():
            own(t + 2)

        @pl.when(t + 1 < NQ)
        def _():
            forward(t + 1)

        opposite(t)
        wait_bytes(g.at[q, :, pl.ds(0, 4)], s_recv.at[t])

        @pl.when(t == 0)
        def _():
            cw = column_weights(q)
            scaled[0:HID, :] = (cw * h[...].astype(F32)).astype(BF16)
            scaled[HID:HPAD, :] = jnp.zeros((HPAD - HID, COLS), BF16)

        part = dot_nn(scaled[...], g[q].reshape(COLS, QW)).T
        t_ref[2 * q] = part[0:PBLK]
        t_ref[2 * q + 1] = part[PBLK:QW]

        @pl.when(t == 0)
        def _():
            sp[0] = t_ref[lax.rem(z + 8, NZ)].astype(BF16)
            plus_send(0).start()

        @pl.when(t == 1)
        def _():
            sm[0] = t_ref[lax.rem(z + 9, NZ)].astype(BF16)
            minus_send(0).start()

        @pl.when(t >= 2)
        def _():
            plus(t - 1)
            minus(t - 1)

        for n in range(NE):
            acc[:, n * 256:(n + 1) * 256] += dot_nt(wq[q], g[q, n].reshape(256, QW))

    cw = column_weights(order(0))
    lane = lax.broadcasted_iota(jnp.int32, (1, 128), 1) // CAP
    sums = []
    for n in range(2 * NE):
        cols = slice(n * 128, (n + 1) * 128)
        image = acc[:, cols]
        sums.append(jnp.sum(h[:, cols].astype(F32) * image, axis=0, keepdims=True))
    table = jnp.concatenate(sums, axis=0)
    turned = [table] + [pltpu.roll(table, CAP * d, 1) for d in range(1, 4)]
    for i in range(NJ):
        line = jnp.zeros((1, 128), F32)
        for n in range(NE):
            src = turned[(n - i) % 4][2 * n + i // 4:2 * n + i // 4 + 1, :]
            line = jnp.where(lane == n, src, line)
        rs[i] = jnp.broadcast_to(line, (8, 128))
    rr[j] = rs[j]

    def r1(d):
        to = lax.rem(j + d, NJ)
        return pltpu.make_async_remote_copy(
            src_ref=rs.at[to], dst_ref=rr.at[j], send_sem=r1_send.at[d - 1], recv_sem=r1_recv.at[d - 1],
            device_id=(z, y * NJ + to), device_id_type=MESH,
        )

    for d in range(1, NJ):
        r1(d).start()

    gh[...] = (cw * acc[...]).astype(BF16)
    cp_gh = pltpu.make_async_copy(gh, gh_hbm, out_sem)
    cp_gh.start()

    plus(7)

    for d in range(1, NJ):
        r1(d).wait_recv()
    total = rr[0]
    for i in range(1, NJ):
        total = total + rr[i]
    ri[y] = total

    def r2(d):
        to = lax.rem(y + d, NE)
        return pltpu.make_async_remote_copy(
            src_ref=ri.at[y], dst_ref=ri.at[y], send_sem=r2_send.at[d - 1], recv_sem=r2_recv.at[d - 1],
            device_id=(z, to * NJ + j), device_id_type=MESH,
        )

    for d in range(1, NE):
        r2(d).start()

    wait_bytes(rm.at[6], rm_recv.at[6])
    partial = t_ref[z] + rm[6].astype(F32)

    for d in range(1, NE):
        r2(d).wait_recv()
    lanes = lax.broadcasted_iota(jnp.int32, (8, 128), 1) // CAP
    subl = lax.broadcasted_iota(jnp.int32, (8, 128), 0)
    inner = jnp.zeros((8, 128), F32)
    for e in range(NE):
        moved = pltpu.roll(ri[e], lax.rem(CAP * (e + NE - y), 128), 1)
        inner = jnp.where((lanes == e) & (subl == e), moved, inner)
    hi = inner.astype(BF16)
    rest = inner - hi.astype(F32)
    mid = rest.astype(BF16)
    low = (rest - mid.astype(F32)).astype(BF16)
    selected = sel[...]
    found = dot_nn(hi, selected) + dot_nn(mid, selected) + dot_nn(low, selected)
    dprob = jnp.zeros((4, TOK), F32)
    for e in range(NE):
        dprob = dprob + jnp.where((ids == e) & live, found[e:e + 1, :], 0.0)
    gl_ref[...] = probs * (dprob - jnp.sum(probs * dprob, axis=0, keepdims=True))

    wait_bytes(rp.at[7], rp_recv.at[7])
    final = partial + rp[7].astype(F32)
    gd_ref[...] = final[0:BLK, 0:HID].astype(BF16)

    @pl.loop(0, NQ)
    def _(t):
        for d in range(1, NE):
            y_copy(t, d).wait_send()
        for kind in range(4):
            x_copy(t, kind).wait_send()
            s_copy(t, kind).wait_send()
        plus_send(t).wait_send()

    @pl.loop(0, NQ - 1)
    def _(t):
        minus_send(t).wait_send()

    for d in range(1, NJ):
        r1(d).wait_send()
    for d in range(1, NE):
        r2(d).wait_send()
    cp_gh.wait()


def body(upstream, router_logits, expert_ids, guard_mask, w_down, saved_hidden):
    dma = pltpu.SemaphoreType.DMA
    vmem = pl.BlockSpec(memory_space=pltpu.VMEM)
    anywhere = pl.BlockSpec(memory_space=pl.ANY)
    gh, gd, gl = pl.pallas_call(
        kernel,
        out_shape=(
            jax.ShapeDtypeStruct((HID, COLS), BF16),
            jax.ShapeDtypeStruct((BLK, HID), BF16),
            jax.ShapeDtypeStruct((4, TOK), F32),
        ),
        in_specs=[anywhere, vmem, vmem, vmem, anywhere, anywhere],
        out_specs=(anywhere, vmem, vmem),
        scratch_shapes=[
            pltpu.VMEM((D, TOK), BF16),
            pltpu.VMEM((D, TOK), F32),
            pltpu.VMEM((HID, D), BF16),
            pltpu.VMEM((NQ, HID, QW), BF16),
            pltpu.VMEM((HID, COLS), BF16),
            pltpu.VMEM((HPAD, COLS), BF16),
            pltpu.VMEM((NQ, TOK, QW), BF16),
            pltpu.VMEM((NQ, NE, NJ, CAP, QW), BF16),
            pltpu.VMEM((HID, COLS), F32),
            pltpu.VMEM((HID, COLS), BF16),
            pltpu.VMEM((NZ, PBLK, HPAD), F32),
            pltpu.VMEM((8, PBLK, HPAD), BF16),
            pltpu.VMEM((8, PBLK, HPAD), BF16),
            pltpu.VMEM((8, PBLK, HPAD), BF16),
            pltpu.VMEM((8, PBLK, HPAD), BF16),
            pltpu.VMEM((TOK, TOK), BF16),
            pltpu.VMEM((NJ, 8, 128), F32),
            pltpu.VMEM((NJ, 8, 128), F32),
            pltpu.VMEM((NE, 8, 128), F32),
            dma((3,)),
            dma((NQ, 3)), dma((NQ,)),
            dma((NQ, 4)), dma((NQ,)), dma((NQ,)), dma((NQ,)),
            dma((NQ, 4)), dma((NQ,)),
            dma((8,)), dma((8,)), dma((8,)), dma((8,)),
            dma((7,)), dma((7,)), dma((3,)), dma((3,)),
            dma,
        ],
        compiler_params=pltpu.CompilerParams(
            collective_id=0, has_side_effects=True, vmem_limit_bytes=50 * 1024 * 1024
        ),
    )(upstream.T, expert_ids.T, router_logits.T, guard_mask.reshape(1, TOK), w_down, saved_hidden)
    return gh, gd, gl.T


def solution(mesh):
    in_specs = (
        P(("dp", "ep"), None),
        P(("dp", "ep"), None),
        P(("dp", "ep"), None),
        P(("dp", "ep")),
        P("ep", None),
        P("ep", "dp"),
    )
    out_specs = (P("ep", "dp"), P("dp", "ep"), P(("dp", "ep"), None))
    return jax.shard_map(body, mesh=mesh, in_specs=in_specs, out_specs=out_specs, check_vma=False)
```

time: 206 us -> 77.4 us (0.38)
  waiting for transfers between devices: 81.4 us -> 0 us
  Pallas kernels: 0 us -> 70.1 us
  blocking collectives: 60.6 us -> 0 us
  starting transfers between devices: 26.2 us -> 0 us
  matrix products: 17.1 us -> 0 us
  other arithmetic: 6.48 us -> 0 us
  local copies, waits for them, and re-layouts: 10.7 us -> 6.34 us
    all_to_all x3 -> x0, waiting for transfers between devices: 81.4 us -> none  [the longest x1 69.9 us: body(): lax.all_to_all(send_rows, 'ep', split_axis=0, concat_axis=0, tiled=True)]
    pallas_call x0 -> x1, Pallas kernels: none -> 70.1 us  [body(): pl.pallas_call(kernel, out_shape=(jax.ShapeDtypeStruct((HID, COLS), BF16)...]
    unnamed x1 -> x0, blocking collectives: 60.6 us -> none
    all_to_all x3 -> x0, starting transfers between devices: 24.2 us -> none  [the longest x1 11.5 us: body(): lax.all_to_all(send_rows, 'ep', split_axis=0, concat_axis=0, tiled=True)]
    dot_general x3 -> x0, matrix products: 17.1 us -> none  [the longest x1 8.31 us: body(): lax.dot_general(recv_rows, scaled, (((0,), (1,)), ((), ())), preferred_el...]
    unnamed x8 -> x13, local copies, waits for them, and re-layouts: 2.95 us -> 6.34 us
    broadcast_in_dim x1 -> x0, local copies, waits for them, and re-layouts: 3.05 us -> none  [body(): jnp.broadcast_to(send_rows.reshape(EXP_WIN, 1, capacity, width), (EXP_WIN...]
    convert_element_type x4 -> x0, other arithmetic: 2.46 us -> none  [the longest x1 2.4 us: body(): grad_hidden = (recv_weight[None, :] * image).astype(jnp.bfloat16)]
  transfers between devices with their start and end apart: 4 -> 0, of which waited for: 3 -> 0; matrix products, arithmetic and copies ran while one was open for 2% -> 0% of each run, Pallas kernels for 0% -> 0%
where the time goes in v1:
time: 77.4 us; the launch traced here: 77.1 us
  Pallas kernels  70.1 us (91%)
  local copies, waits for them, and re-layouts  6.34 us (8%)
    pallas_call x1, Pallas kernels, body(): pl.pallas_call(kernel, out_shape=(jax.ShapeDtypeStruct((HID, COLS), BF16)...  70.1 us
    unnamed x13, local copies, waits for them, and re-layouts  6.34 us

profile of v1, /device:TPU:1, one launch (start us, length us, event | category | flops | bytes accessed | tf_op | source)
XLA Modules:
  0.0 77.1 jit_solution(3504279355015928690)
XLA Ops:
  0.6 0.0 copy-start
  0.6 1.1 %copy-done = bf16[128,2880]{0,1:T(8,128)(2,1)S(1)} copy-done((bf16[128,2880]{0,1:T(8,128)(2,1)S(1)}, bf16[128,2880]{0,1:T(8,128)(2,1)}, u32[]{:S(2)}) %copy-start) | copy-done | bytes 737304
  1.7 0.0 copy-start.1
  1.8 1.1 %copy-done.1 = bf16[360,1024]{1,0:T(8,128)(2,1)S(1)} copy-done((bf16[360,1024]{1,0:T(8,128)(2,1)S(1)}, bf16[360,1024]{1,0:T(8,128)(2,1)}, u32[]{:S(2)}) %copy-start.1) | copy-done | bytes 737304
  2.9 0.0 copy-start.2
  2.9 0.7 copy-done.2
  3.5 0.0 copy-start.3
  3.5 0.7 copy-done.3
  4.2 0.0 copy-start.4
  4.2 0.7 copy-done.4
  4.9 70.1 %shard_map.85 = (bf16[360,1024]{1,0:T(8,128)(2,1)S(1)}, bf16[180,360]{1,0:T(8,128)(2,1)S(1)}, f32[4,128]{1,0:T(4,128)S(1)}) custom-call(bf16[2880,128]{1,0:T(8,128)(2,1)S(1)} %bitcast.5, s32[4,128]{1,0:T(4,128)S(1)} %bitcast.6, f32[4,128]{1,0:T(4,128)S(1)} %bitcast.7, s32[1,128]{1,0:T(1,128)S(1)} %bitcast.9, bf16[360,2880]{1,0:T(8,128)(2,1)} %w_hbm.1, ...), custom_call_target="tpu_custom_call" | custom-call | tf_op jit(solution)/shard_map/pallas_call | solution.py:378
  75.0 0.9 %copy.12 = bf16[360,1024]{1,0:T(8,128)(2,1)} copy(bf16[360,1024]{1,0:T(8,128)(2,1)S(1)} %get-tuple-element.12) | data formatting | bytes 1474560
  75.9 0.7 copy.13
  76.5 0.6 copy.14
Async XLA Ops:
  0.6 1.1 %copy-start = (bf16[128,2880]{0,1:T(8,128)(2,1)S(1)}, bf16[128,2880]{0,1:T(8,128)(2,1)}, u32[]{:S(2)}) copy-start(bf16[128,2880]{0,1:T(8,128)(2,1)} %param.6) | copy-start | bytes 2211844
  1.7 1.1 %copy-start.1 = (bf16[360,1024]{1,0:T(8,128)(2,1)S(1)}, bf16[360,1024]{1,0:T(8,128)(2,1)}, u32[]{:S(2)}) copy-start(bf16[360,1024]{1,0:T(8,128)(2,1)} %h_hbm.1) | copy-start | bytes 2211844
  2.9 0.7 copy-start.2
  3.5 0.7 copy-start.3
  4.2 0.7 copy-start.4

commit v2 on v1

v2 whole, which is shorter than its diff:
```python
import jax
import jax.numpy as jnp
from jax import lax
from jax.experimental import pallas as pl
from jax.experimental.pallas import tpu as pltpu
from jax.sharding import PartitionSpec as P

MESH = pl.DeviceIdType.MESH
F32 = jnp.float32
BF16 = jnp.bfloat16

NE = 4
NX = 4
NJ = 8
NZ = 16
CAP = 32
TOK = 128
D = 2880
BLK = 180
PBLK = 192
NQ = 8
QW = 2 * PBLK
HID = 360
HPAD = 384
COLS = 1024
HALF = PBLK // 2
WLANE = BLK


def dot_nt(a, b):
    return lax.dot_general(a, b, (((1,), (1,)), ((), ())), preferred_element_type=F32)


def dot_nn(a, b):
    return lax.dot_general(a, b, (((1,), (0,)), ((), ())), preferred_element_type=F32)


def kernel(
    up_hbm, ids_hbm, logits_hbm, guard_hbm, w_hbm, h_hbm,
    gh_hbm, gd_hbm, gl_hbm,
    ids_ref, logits_ref, guard_ref, gd, gl, up, upf, upb, w, wblk, wq, h, scaled, cws, rows, g, acc, gh,
    t_ref, sp, sm, rp, rm, sel, rs, rr, ri,
    in_sem, y_send, y_recv, x_send, xl_recv, xr_recv, xo_recv, s_send, s_recv,
    sp_send, rp_recv, sm_send, rm_recv, r1_send, r1_recv, r2_send, r2_recv, out_sem,
):
    z = lax.axis_index("dp")
    ep = lax.axis_index("ep")
    y = ep // NJ
    j = ep % NJ
    x = j // 2
    c = j % 2
    zr = lax.rem(z + 1, NZ)
    zl = lax.rem(z + NZ - 1, NZ)
    jr = lax.rem(x + 1, NX) * 2 + c
    jl = lax.rem(x + NX - 1, NX) * 2 + c
    jo = lax.rem(x + 2, NX) * 2 + c
    js = x * 2 + (1 - c)

    cp_small = [
        pltpu.make_async_copy(ids_hbm, ids_ref, in_sem.at[3]),
        pltpu.make_async_copy(logits_hbm, logits_ref, in_sem.at[4]),
        pltpu.make_async_copy(guard_hbm, guard_ref, in_sem.at[5]),
    ]
    cp_up = pltpu.make_async_copy(up_hbm, up, in_sem.at[0])
    cp_h = pltpu.make_async_copy(h_hbm, h, in_sem.at[1])
    cp_w = pltpu.make_async_copy(w_hbm, w, in_sem.at[2])
    for cp in cp_small:
        cp.start()
    cp_up.start()
    cp_w.start()
    cp_h.start()

    barrier = pltpu.get_barrier_semaphore()
    for d in range(1, NJ):
        pl.semaphore_signal(barrier, 1, device_id=(z, y * NJ + lax.rem(j + d, NJ)), device_id_type=MESH)
    for d in range(1, NE):
        pl.semaphore_signal(barrier, 1, device_id=(z, lax.rem(y + d, NE) * NJ + j), device_id_type=MESH)
    pl.semaphore_signal(barrier, 1, device_id=(zr, ep), device_id_type=MESH)
    pl.semaphore_signal(barrier, 1, device_id=(zl, ep), device_id_type=MESH)

    for cp in cp_small:
        cp.wait()
    ids = ids_ref[...]
    logits = logits_ref[...]
    live = guard_ref[...] == 1
    top = jnp.max(logits, axis=0, keepdims=True)
    ex = jnp.exp(logits - top)
    probs = ex / jnp.sum(ex, axis=0, keepdims=True)
    combine = probs.astype(BF16).astype(F32)
    chosen = []
    weight = []
    for e in range(NE):
        hit = ((ids == e) & live).astype(F32)
        chosen.append(jnp.sum(hit, axis=0, keepdims=True))
        weight.append(jnp.sum(hit * combine, axis=0, keepdims=True))
    mask = jnp.concatenate(chosen + [jnp.zeros((8 - NE, TOK), F32)], axis=0)
    earlier = (
        lax.broadcasted_iota(jnp.int32, (TOK, TOK), 0) < lax.broadcasted_iota(jnp.int32, (TOK, TOK), 1)
    ).astype(F32).astype(BF16)
    slot = dot_nn(mask.astype(BF16), earlier)
    place = lax.broadcasted_iota(jnp.int32, (CAP, TOK), 0).astype(F32)
    picks = []
    wcols = []
    for e in range(NE):
        pick = jnp.where(slot[e:e + 1, :] == place, mask[e:e + 1, :], 0.0)
        picks.append(pick)
        wcols.append(jnp.sum(pick * weight[e], axis=1, keepdims=True))
    select = jnp.concatenate(picks, axis=0).astype(BF16)
    wcol = jnp.concatenate(wcols, axis=0)
    sel[...] = select
    at_weight = lax.broadcasted_iota(jnp.int32, (TOK, QW), 1) == WLANE

    cp_up.wait()
    upf[...] = up[...].astype(F32)
    gap = jnp.zeros((PBLK - BLK, TOK), F32)
    for b in range(NZ):
        upb[b] = jnp.concatenate([upf[b * BLK:(b + 1) * BLK, :], gap], axis=0).astype(BF16)

    def first(t):
        return lax.rem(z + 8 - t + NZ, NZ)

    def second(t):
        return lax.rem(z + 9 + t, NZ)

    def make_rows(t):
        part = jnp.concatenate([upb[first(t)], upb[second(t)]], axis=0)
        got = dot_nt(sel[...], part)
        rows[t] = jnp.where(at_weight, wcol, got).astype(BF16)
        g[t, 0, j] = rows[t, pl.ds(pl.multiple_of(y * CAP, CAP), CAP), :]

    def y_copy(t, d):
        e = lax.rem(y + d, NE)
        return pltpu.make_async_remote_copy(
            src_ref=rows.at[t, pl.ds(pl.multiple_of(e * CAP, CAP), CAP)],
            dst_ref=g.at[t, NE - d, j],
            send_sem=y_send.at[t, d - 1],
            recv_sem=y_recv.at[t],
            device_id=(z, e * NJ + j),
            device_id_type=MESH,
        )

    def x_copy(t, kind):
        ref, to, sem = [
            (g.at[t, 0, j], jr, xl_recv),
            (g.at[t, 0, j], jl, xr_recv),
            (g.at[t, pl.ds(1, 3), j], jr, xl_recv),
            (g.at[t, pl.ds(1, 3), j], jl, xr_recv),
            (g.at[t, pl.ds(0, 2), jl], jr, xo_recv),
            (g.at[t, pl.ds(2, 2), jr], jl, xo_recv),
        ][kind]
        return pltpu.make_async_remote_copy(
            src_ref=ref, dst_ref=ref, send_sem=x_send.at[t, kind], recv_sem=sem.at[t],
            device_id=(z, y * NJ + to), device_id_type=MESH,
        )

    def s_copy(t, kind):
        ref = [
            g.at[t, 0, j],
            g.at[t, pl.ds(1, 3), j],
            g.at[t, :, jl],
            g.at[t, :, jr],
            g.at[t, :, jo],
        ][kind]
        return pltpu.make_async_remote_copy(
            src_ref=ref, dst_ref=ref, send_sem=s_send.at[t, kind], recv_sem=s_recv.at[t],
            device_id=(z, y * NJ + js), device_id_type=MESH,
        )

    def wait_bytes(ref, sem):
        pltpu.make_async_copy(ref, ref, sem).wait()

    def start(t):
        for d in (2, 1, 3):
            y_copy(t, d).start()
        x_copy(t, 0).start()
        x_copy(t, 1).start()
        s_copy(t, 0).start()

    def rest(t):
        wait_bytes(g.at[t, pl.ds(1, 3), j], y_recv.at[t])
        x_copy(t, 2).start()
        x_copy(t, 3).start()
        s_copy(t, 1).start()

    def forward(t):
        wait_bytes(g.at[t, :, jl], xl_recv.at[t])
        x_copy(t, 4).start()
        s_copy(t, 2).start()
        wait_bytes(g.at[t, :, jr], xr_recv.at[t])
        x_copy(t, 5).start()
        s_copy(t, 3).start()

    def opposite(t):
        wait_bytes(g.at[t, :, jo], xo_recv.at[t])
        s_copy(t, 4).start()

    make_rows(0)
    pl.semaphore_wait(barrier, NJ - 1 + NE - 1 + 2)
    start(0)
    make_rows(1)
    start(1)
    make_rows(2)
    start(2)

    cp_w.wait()
    wgap = jnp.zeros((HID, PBLK - BLK), BF16)
    for b in range(NZ):
        wblk[b] = jnp.concatenate([w[:, b * BLK:(b + 1) * BLK], wgap], axis=1)

    def pair_w(t):
        wq[t] = jnp.concatenate([wblk[first(t)], wblk[second(t)]], axis=1)

    pair_w(0)
    rest(0)
    make_rows(3)
    start(3)
    rest(1)
    acc[...] = jnp.zeros_like(acc)
    pair_w(1)
    forward(0)
    make_rows(4)
    start(4)
    rest(2)
    cp_h.wait()
    forward(1)

    def plus_send(t, half):
        at = pl.ds(half * HALF, HALF)
        return pltpu.make_async_remote_copy(
            src_ref=sp.at[t, at], dst_ref=rp.at[t, at], send_sem=sp_send.at[t, half], recv_sem=rp_recv.at[t, half],
            device_id=(zr, ep), device_id_type=MESH,
        )

    def minus_send(t, half):
        at = pl.ds(half * HALF, HALF)
        return pltpu.make_async_remote_copy(
            src_ref=sm.at[t, at], dst_ref=rm.at[t, at], send_sem=sm_send.at[t, half], recv_sem=rm_recv.at[t, half],
            device_id=(zl, ep), device_id_type=MESH,
        )

    def chains(t, half):
        at = slice(half * HALF, (half + 1) * HALF)

        @pl.when(t == 0)
        def _():
            sp[t, at, :] = t_ref[at, :].astype(BF16)
            sm[t, at, :] = t_ref[PBLK + at.start:PBLK + at.stop, :].astype(BF16)

        @pl.when(t > 0)
        def _():
            ref = rp.at[t - 1, pl.ds(half * HALF, HALF)]
            wait_bytes(ref, rp_recv.at[t - 1, half])
            sp[t, at, :] = (t_ref[at, :] + rp[t - 1, at, :].astype(F32)).astype(BF16)

        plus_send(t, half).start()

        @pl.when((t > 0) & (t < NQ - 1))
        def _():
            ref = rm.at[t - 1, pl.ds(half * HALF, HALF)]
            wait_bytes(ref, rm_recv.at[t - 1, half])
            sm[t, at, :] = (t_ref[PBLK + at.start:PBLK + at.stop, :] + rm[t - 1, at, :].astype(F32)).astype(BF16)

        @pl.when(t < NQ - 1)
        def _():
            minus_send(t, half).start()

    def source(n):
        return lax.rem(n - y + NE, NE)

    def scale_columns():
        one = (lax.broadcasted_iota(jnp.int32, (8, 128), 1) == WLANE - 128).astype(F32).astype(BF16)
        for n in range(NE):
            dy = source(n)
            cols = slice(n * 256, (n + 1) * 256)
            cw = dot_nt(one, g[0, dy, :, :, 128:256].reshape(256, 128))
            cws[:, cols] = cw
            scaled[dy, 0:HID, :] = (cw[0:1, :] * h[:, cols].astype(F32)).astype(BF16)
            scaled[dy, HID:HPAD, :] = jnp.zeros((HPAD - HID, 256), BF16)

    def r1(d):
        to = lax.rem(j + d, NJ)
        return pltpu.make_async_remote_copy(
            src_ref=rs.at[to], dst_ref=rr.at[j], send_sem=r1_send.at[d - 1], recv_sem=r1_recv.at[d - 1],
            device_id=(z, y * NJ + to), device_id_type=MESH,
        )

    def inner_products():
        lane = lax.broadcasted_iota(jnp.int32, (1, 128), 1) // CAP
        sums = []
        for n in range(2 * NE):
            cols = slice(n * 128, (n + 1) * 128)
            sums.append(jnp.sum(h[:, cols].astype(F32) * acc[:, cols], axis=0, keepdims=True))
        table = jnp.concatenate(sums, axis=0)
        turned = [table] + [pltpu.roll(table, CAP * d, 1) for d in range(1, 4)]
        for i in range(NJ):
            line = jnp.zeros((1, 128), F32)
            for n in range(NE):
                src = turned[(n - i) % 4][2 * n + i // 4:2 * n + i // 4 + 1, :]
                line = jnp.where(lane == n, src, line)
            rs[i] = jnp.broadcast_to(line, (8, 128))
        for d in range(1, NJ):
            r1(d).start()
        rr[j] = rs[j]

    @pl.loop(0, NQ)
    def _(t):
        opposite(t)

        @pl.when(t + 5 < NQ)
        def _():
            make_rows(t + 5)
            start(t + 5)

        @pl.when(t + 3 < NQ)
        def _():
            rest(t + 3)

        @pl.when(t + 2 < NQ)
        def _():
            pair_w(t + 2)
            forward(t + 2)

        @pl.when(t > 0)
        def _():
            chains(t - 1, 1)

        wait_bytes(g.at[t, :, pl.ds(0, 4)], s_recv.at[t])

        @pl.when(t == 0)
        def _():
            scale_columns()

        for n in range(NE):
            acc[:, n * 256:(n + 1) * 256] += dot_nt(wq[t], g[t, source(n)].reshape(256, QW))

        @pl.when(t == NQ - 1)
        def _():
            inner_products()

        part = dot_nn(scaled[0], g[t, 0].reshape(256, QW))
        for dy in range(1, NE):
            part = part + dot_nn(scaled[dy], g[t, dy].reshape(256, QW))
        t_ref[...] = part.T
        chains(t, 0)

    chains(NQ - 1, 1)

    gh[...] = (cws[0:1, :] * acc[...]).astype(BF16)
    cp_gh = pltpu.make_async_copy(gh, gh_hbm, out_sem.at[0])
    cp_gh.start()

    for d in range(1, NJ):
        r1(d).wait_recv()
    total = rr[0]
    for i in range(1, NJ):
        total = total + rr[i]
    ri[y] = total

    def r2(d):
        to = lax.rem(y + d, NE)
        return pltpu.make_async_remote_copy(
            src_ref=ri.at[y], dst_ref=ri.at[y], send_sem=r2_send.at[d - 1], recv_sem=r2_recv.at[d - 1],
            device_id=(z, to * NJ + j), device_id_type=MESH,
        )

    for d in range(1, NE):
        r2(d).start()

    @pl.loop(0, NQ)
    def _(t):
        for d in range(1, NE):
            y_copy(t, d).wait_send()
        for kind in range(6):
            x_copy(t, kind).wait_send()
        for kind in range(5):
            s_copy(t, kind).wait_send()

    for half in range(2):
        wait_bytes(rm.at[NQ - 2, pl.ds(half * HALF, HALF)], rm_recv.at[NQ - 2, half])
    t_ref[0:PBLK, :] = t_ref[PBLK:QW, :] + rm[NQ - 2].astype(F32)

    for d in range(1, NE):
        r2(d).wait_recv()
    lanes = lax.broadcasted_iota(jnp.int32, (8, 128), 1) // CAP
    subl = lax.broadcasted_iota(jnp.int32, (8, 128), 0)
    inner = jnp.zeros((8, 128), F32)
    for e in range(NE):
        moved = pltpu.roll(ri[e], lax.rem(CAP * (e + NE - y), 128), 1)
        inner = jnp.where((lanes == e) & (subl == e), moved, inner)
    hi = inner.astype(BF16)
    rem = inner - hi.astype(F32)
    mid = rem.astype(BF16)
    low = (rem - mid.astype(F32)).astype(BF16)
    selected = sel[...]
    found = dot_nn(hi, selected) + dot_nn(mid, selected) + dot_nn(low, selected)
    dprob = jnp.zeros((4, TOK), F32)
    for e in range(NE):
        dprob = dprob + jnp.where((ids == e) & live, found[e:e + 1, :], 0.0)
    gl[...] = probs * (dprob - jnp.sum(probs * dprob, axis=0, keepdims=True))
    cp_gl = pltpu.make_async_copy(gl, gl_hbm, out_sem.at[1])
    cp_gl.start()

    for half in range(2):
        wait_bytes(rp.at[NQ - 1, pl.ds(half * HALF, HALF)], rp_recv.at[NQ - 1, half])
    final = t_ref[0:PBLK, :] + rp[NQ - 1].astype(F32)
    gd[...] = final[0:BLK, 0:HID].astype(BF16)
    cp_gd = pltpu.make_async_copy(gd, gd_hbm, out_sem.at[2])
    cp_gd.start()

    @pl.loop(0, NQ - 1)
    def _(t):
        for half in range(2):
            plus_send(t, half).wait_send()
            minus_send(t, half).wait_send()

    for half in range(2):
        plus_send(NQ - 1, half).wait_send()
    for d in range(1, NJ):
        r1(d).wait_send()
    for d in range(1, NE):
        r2(d).wait_send()
    cp_gh.wait()
    cp_gl.wait()
    cp_gd.wait()


def hand_over(gh_in, gd_in, gl_in, gh_out, gd_out, gl_out, gh, gd, gl, sem):
    refs = [(gh_in, gh, gh_out), (gd_in, gd, gd_out), (gl_in, gl, gl_out)]
    for i, (a, b, _) in enumerate(refs):
        pltpu.make_async_copy(a, b, sem.at[0, i]).start()
    for i, (a, b, o) in enumerate(refs):
        pltpu.make_async_copy(a, b, sem.at[0, i]).wait()
        pltpu.make_async_copy(b, o, sem.at[1, i]).start()
    for i, (_, b, o) in enumerate(refs):
        pltpu.make_async_copy(b, o, sem.at[1, i]).wait()


def body(upstream, router_logits, expert_ids, guard_mask, w_down, saved_hidden):
    dma = pltpu.SemaphoreType.DMA
    hbm = pl.BlockSpec(memory_space=pltpu.HBM)
    outs = (
        jax.ShapeDtypeStruct((HID, COLS), BF16),
        jax.ShapeDtypeStruct((BLK, HID), BF16),
        jax.ShapeDtypeStruct((4, TOK), F32),
    )
    results = pl.pallas_call(
        kernel,
        out_shape=outs,
        in_specs=[hbm] * 6,
        out_specs=(hbm, hbm, hbm),
        scratch_shapes=[
            pltpu.VMEM((4, TOK), jnp.int32),
            pltpu.VMEM((4, TOK), F32),
            pltpu.VMEM((1, TOK), jnp.int32),
            pltpu.VMEM((BLK, HID), BF16),
            pltpu.VMEM((4, TOK), F32),
            pltpu.VMEM((D, TOK), BF16),
            pltpu.VMEM((D, TOK), F32),
            pltpu.VMEM((NZ, PBLK, TOK), BF16),
            pltpu.VMEM((HID, D), BF16),
            pltpu.VMEM((NZ, HID, PBLK), BF16),
            pltpu.VMEM((NQ, HID, QW), BF16),
            pltpu.VMEM((HID, COLS), BF16),
            pltpu.VMEM((NE, HPAD, 256), BF16),
            pltpu.VMEM((8, COLS), F32),
            pltpu.VMEM((NQ, TOK, QW), BF16),
            pltpu.VMEM((NQ, NE, NJ, CAP, QW), BF16),
            pltpu.VMEM((HID, COLS), F32),
            pltpu.VMEM((HID, COLS), BF16),
            pltpu.VMEM((QW, HPAD), F32),
            pltpu.VMEM((NQ, PBLK, HPAD), BF16),
            pltpu.VMEM((NQ, PBLK, HPAD), BF16),
            pltpu.VMEM((NQ, PBLK, HPAD), BF16),
            pltpu.VMEM((NQ, PBLK, HPAD), BF16),
            pltpu.VMEM((TOK, TOK), BF16),
            pltpu.VMEM((NJ, 8, 128), F32),
            pltpu.VMEM((NJ, 8, 128), F32),
            pltpu.VMEM((NE, 8, 128), F32),
            dma((6,)),
            dma((NQ, 3)), dma((NQ,)),
            dma((NQ, 6)), dma((NQ,)), dma((NQ,)), dma((NQ,)),
            dma((NQ, 5)), dma((NQ,)),
            dma((NQ, 2)), dma((NQ, 2)), dma((NQ, 2)), dma((NQ, 2)),
            dma((7,)), dma((7,)), dma((3,)), dma((3,)),
            dma((3,)),
        ],
        compiler_params=pltpu.CompilerParams(
            collective_id=0, has_side_effects=True, vmem_limit_bytes=64 * 1024 * 1024
        ),
    )(upstream.T, expert_ids.T, router_logits.T, guard_mask.reshape(1, TOK), w_down, saved_hidden)
    gh, gd, gl = pl.pallas_call(
        hand_over,
        out_shape=outs,
        in_specs=[hbm] * 3,
        out_specs=(hbm, hbm, hbm),
        scratch_shapes=[
            pltpu.VMEM((HID, COLS), BF16),
            pltpu.VMEM((BLK, HID), BF16),
            pltpu.VMEM((4, TOK), F32),
            dma((2, 3)),
        ],
        compiler_params=pltpu.CompilerParams(vmem_limit_bytes=64 * 1024 * 1024),
    )(*results)
    return gh, gd, gl.T


def solution(mesh):
    in_specs = (
        P(("dp", "ep"), None),
        P(("dp", "ep"), None),
        P(("dp", "ep"), None),
        P(("dp", "ep")),
        P("ep", None),
        P("ep", "dp"),
    )
    out_specs = (P("ep", "dp"), P("dp", "ep"), P(("dp", "ep"), None))
    return jax.shard_map(body, mesh=mesh, in_specs=in_specs, out_specs=out_specs, check_vma=False)
```

time: 77.4 us -> 69.7 us (0.901)
  local copies, waits for them, and re-layouts: 6.34 us -> 0 us
  Pallas kernels: 70.1 us -> 68.9 us
    unnamed x13 -> x0, local copies, waits for them, and re-layouts: 6.34 us -> none
    pallas_call x1 -> x2, Pallas kernels: 70.1 us -> 68.9 us  [the longest x1 66.8 us: body(): pl.pallas_call(kernel, out_shape=outs, in_specs=[hbm] * 6, out_specs=(hbm...]
where the time goes in v2:
time: 69.7 us; the launch traced here: 69.5 us
  Pallas kernels  68.9 us (99%)
    pallas_call x1, Pallas kernels, body(): pl.pallas_call(kernel, out_shape=outs, in_specs=[hbm] * 6, out_specs=(hbm...  66.8 us
    pallas_call x1, Pallas kernels, body(): pl.pallas_call(hand_over, out_shape=outs, in_specs=[hbm] * 3, out_specs=(...  2.07 us

profile of v2, /device:TPU:1, one launch (start us, length us, event | category | flops | bytes accessed | tf_op | source)
XLA Modules:
  0.0 69.5 jit_solution(7695225884230945397)
XLA Ops:
  0.6 66.8 %shard_map.85 = (bf16[360,1024]{1,0:T(8,128)(2,1)}, bf16[180,360]{1,0:T(8,128)(2,1)}, f32[4,128]{1,0:T(4,128)}) custom-call(bf16[2880,128]{1,0:T(8,128)(2,1)} %bitcast.5, s32[4,128]{1,0:T(4,128)} %bitcast.6, f32[4,128]{1,0:T(4,128)} %bitcast.7, s32[1,128]{1,0:T(1,128)} %bitcast.8, bf16[360,2880]{1,0:T(8,128)(2,1)} %w_hbm.1, bf16[360,1024]{1,0:T(8,128)(2,1)} %h_hbm.1), custom_call_target="tpu_custom_call" | custom-call | tf_op jit(solution)/shard_map/pallas_call | solution.py:446
  67.5 2.1 %shard_map.86 = (bf16[360,1024]{1,0:T(8,128)(2,1)}, bf16[180,360]{1,0:T(8,128)(2,1)}, f32[4,128]{1,0:T(4,128)}) custom-call(bf16[360,1024]{1,0:T(8,128)(2,1)} %get-tuple-element.9.gh_in, bf16[180,360]{1,0:T(8,128)(2,1)} %get-tuple-element.10.gd_in, f32[4,128]{1,0:T(4,128)} %get-tuple-element.11.gl_in), custom_call_target="tpu_custom_call" | custom-call | tf_op jit(solution)/shard_map/pallas_call | solution.py:491

commit v3 on v2

--- a/solution.py
+++ b/solution.py
@@ -23,7 +23,8 @@
 HID = 360
 HPAD = 384
 COLS = 1024
-HALF = PBLK // 2
+CUTS = 4
+PART = PBLK // CUTS
 WLANE = BLK
 
 
@@ -37,11 +38,11 @@
 
 def kernel(
     up_hbm, ids_hbm, logits_hbm, guard_hbm, w_hbm, h_hbm,
-    gh_hbm, gd_hbm, gl_hbm,
-    ids_ref, logits_ref, guard_ref, gd, gl, up, upf, upb, w, wblk, wq, h, scaled, cws, rows, g, acc, gh,
+    gh, gd, gl,
+    ids_ref, logits_ref, guard_ref, up, upf, upb, w, wblk, wq, h, scaled, cws, rows, g, acc,
     t_ref, sp, sm, rp, rm, sel, rs, rr, ri,
     in_sem, y_send, y_recv, x_send, xl_recv, xr_recv, xo_recv, s_send, s_recv,
-    sp_send, rp_recv, sm_send, rm_recv, r1_send, r1_recv, r2_send, r2_recv, out_sem,
+    sp_send, rp_recv, sm_send, rm_recv, r1_send, r1_recv, r2_send, r2_recv,
 ):
     z = lax.axis_index("dp")
     ep = lax.axis_index("ep")
@@ -224,45 +225,42 @@
     cp_h.wait()
     forward(1)
 
-    def plus_send(t, half):
-        at = pl.ds(half * HALF, HALF)
-        return pltpu.make_async_remote_copy(
-            src_ref=sp.at[t, at], dst_ref=rp.at[t, at], send_sem=sp_send.at[t, half], recv_sem=rp_recv.at[t, half],
+    def plus_send(t, k):
+        at = pl.ds(k * PART, PART)
+        return pltpu.make_async_remote_copy(
+            src_ref=sp.at[t, at], dst_ref=rp.at[t, at], send_sem=sp_send.at[t, k], recv_sem=rp_recv.at[t, k],
             device_id=(zr, ep), device_id_type=MESH,
         )
 
-    def minus_send(t, half):
-        at = pl.ds(half * HALF, HALF)
-        return pltpu.make_async_remote_copy(
-            src_ref=sm.at[t, at], dst_ref=rm.at[t, at], send_sem=sm_send.at[t, half], recv_sem=rm_recv.at[t, half],
+    def minus_send(t, k):
+        at = pl.ds(k * PART, PART)
+        return pltpu.make_async_remote_copy(
+            src_ref=sm.at[t, at], dst_ref=rm.at[t, at], send_sem=sm_send.at[t, k], recv_sem=rm_recv.at[t, k],
             device_id=(zl, ep), device_id_type=MESH,
         )
 
-    def chains(t, half):
-        at = slice(half * HALF, (half + 1) * HALF)
+    def chains(t, k):
+        at = slice(k * PART, (k + 1) * PART)
+        at2 = slice(PBLK + k * PART, PBLK + (k + 1) * PART)
 
         @pl.when(t == 0)
         def _():
             sp[t, at, :] = t_ref[at, :].astype(BF16)
-            sm[t, at, :] = t_ref[PBLK + at.start:PBLK + at.stop, :].astype(BF16)
+            plus_send(t, k).start()
+            sm[t, at, :] = t_ref[at2, :].astype(BF16)
+            minus_send(t, k).start()
 
         @pl.when(t > 0)
         def _():
-            ref = rp.at[t - 1, pl.ds(half * HALF, HALF)]
-            wait_bytes(ref, rp_recv.at[t - 1, half])
+            wait_bytes(rp.at[t - 1, pl.ds(k * PART, PART)], rp_recv.at[t - 1, k])
             sp[t, at, :] = (t_ref[at, :] + rp[t - 1, at, :].astype(F32)).astype(BF16)
-
-        plus_send(t, half).start()
+            plus_send(t, k).start()
 
         @pl.when((t > 0) & (t < NQ - 1))
         def _():
-            ref = rm.at[t - 1, pl.ds(half * HALF, HALF)]
-            wait_bytes(ref, rm_recv.at[t - 1, half])
-            sm[t, at, :] = (t_ref[PBLK + at.start:PBLK + at.stop, :] + rm[t - 1, at, :].astype(F32)).astype(BF16)
-
-        @pl.when(t < NQ - 1)
-        def _():
-            minus_send(t, half).start()
+            wait_bytes(rm.at[t - 1, pl.ds(k * PART, PART)], rm_recv.at[t - 1, k])
+            sm[t, at, :] = (t_ref[at2, :] + rm[t - 1, at, :].astype(F32)).astype(BF16)
+            minus_send(t, k).start()
 
     def source(n):
         return lax.rem(n - y + NE, NE)
@@ -315,6 +313,10 @@
         def _():
             rest(t + 3)
 
+        @pl.when(t > 0)
+        def _():
+            chains(t - 1, 1)
+
         @pl.when(t + 2 < NQ)
         def _():
             pair_w(t + 2)
@@ -322,7 +324,7 @@
 
         @pl.when(t > 0)
         def _():
-            chains(t - 1, 1)
+            chains(t - 1, 2)
 
         wait_bytes(g.at[t, :, pl.ds(0, 4)], s_recv.at[t])
 
@@ -336,6 +338,10 @@
         @pl.when(t == NQ - 1)
         def _():
             inner_products()
+
+        @pl.when(t > 0)
+        def _():
+            chains(t - 1, 3)
 
         part = dot_nn(scaled[0], g[t, 0].reshape(256, QW))
         for dy in range(1, NE):
@@ -343,11 +349,10 @@
         t_ref[...] = part.T
         chains(t, 0)
 
-    chains(NQ - 1, 1)
+    for k in range(1, CUTS):
+        chains(NQ - 1, k)
 
     gh[...] = (cws[0:1, :] * acc[...]).astype(BF16)
-    cp_gh = pltpu.make_async_copy(gh, gh_hbm, out_sem.at[0])
-    cp_gh.start()
 
     for d in range(1, NJ):
         r1(d).wait_recv()
@@ -375,8 +380,8 @@
         for kind in range(5):
             s_copy(t, kind).wait_send()
 
-    for half in range(2):
-        wait_bytes(rm.at[NQ - 2, pl.ds(half * HALF, HALF)], rm_recv.at[NQ - 2, half])
+    for k in range(CUTS):
+        wait_bytes(rm.at[NQ - 2, pl.ds(k * PART, PART)], rm_recv.at[NQ - 2, k])
     t_ref[0:PBLK, :] = t_ref[PBLK:QW, :] + rm[NQ - 2].astype(F32)
 
     for d in range(1, NE):
@@ -397,46 +402,40 @@
     for e in range(NE):
         dprob = dprob + jnp.where((ids == e) & live, found[e:e + 1, :], 0.0)
     gl[...] = probs * (dprob - jnp.sum(probs * dprob, axis=0, keepdims=True))
-    cp_gl = pltpu.make_async_copy(gl, gl_hbm, out_sem.at[1])
-    cp_gl.start()
-
-    for half in range(2):
-        wait_bytes(rp.at[NQ - 1, pl.ds(half * HALF, HALF)], rp_recv.at[NQ - 1, half])
+
+    for k in range(CUTS):
+        wait_bytes(rp.at[NQ - 1, pl.ds(k * PART, PART)], rp_recv.at[NQ - 1, k])
     final = t_ref[0:PBLK, :] + rp[NQ - 1].astype(F32)
     gd[...] = final[0:BLK, 0:HID].astype(BF16)
-    cp_gd = pltpu.make_async_copy(gd, gd_hbm, out_sem.at[2])
-    cp_gd.start()
 
     @pl.loop(0, NQ - 1)
     def _(t):
-        for half in range(2):
-            plus_send(t, half).wait_send()
-            minus_send(t, half).wait_send()
-
-    for half in range(2):
-        plus_send(NQ - 1, half).wait_send()
+        for k in range(CUTS):
+            plus_send(t, k).wait_send()
+            minus_send(t, k).wait_send()
+
+    for k in range(CUTS):
+        plus_send(NQ - 1, k).wait_send()
     for d in range(1, NJ):
         r1(d).wait_send()
     for d in range(1, NE):
         r2(d).wait_send()
-    cp_gh.wait()
-    cp_gl.wait()
-    cp_gd.wait()
-
-
-def hand_over(gh_in, gd_in, gl_in, gh_out, gd_out, gl_out, gh, gd, gl, sem):
-    refs = [(gh_in, gh, gh_out), (gd_in, gd, gd_out), (gl_in, gl, gl_out)]
-    for i, (a, b, _) in enumerate(refs):
-        pltpu.make_async_copy(a, b, sem.at[0, i]).start()
-    for i, (a, b, o) in enumerate(refs):
-        pltpu.make_async_copy(a, b, sem.at[0, i]).wait()
-        pltpu.make_async_copy(b, o, sem.at[1, i]).start()
-    for i, (_, b, o) in enumerate(refs):
-        pltpu.make_async_copy(b, o, sem.at[1, i]).wait()
+
+
+def hand_over(gh_in, gd_in, gl_in, gh_out, gd_out, gl_out, sem):
+    copies = [
+        pltpu.make_async_copy(a, b, sem.at[i])
+        for i, (a, b) in enumerate([(gh_in, gh_out), (gd_in, gd_out), (gl_in, gl_out)])
+    ]
+    for cp in copies:
+        cp.start()
+    for cp in copies:
+        cp.wait()
 
 
 def body(upstream, router_logits, expert_ids, guard_mask, w_down, saved_hidden):
     dma = pltpu.SemaphoreType.DMA
+    vmem = pl.BlockSpec(memory_space=pltpu.VMEM)
     hbm = pl.BlockSpec(memory_space=pltpu.HBM)
     outs = (
         jax.ShapeDtypeStruct((HID, COLS), BF16),
@@ -445,15 +444,13 @@
     )
     results = pl.pallas_call(
         kernel,
-        out_shape=outs,
+        out_shape=(pltpu.VMEM((HID, COLS), BF16), pltpu.VMEM((BLK, HID), BF16), pltpu.VMEM((4, TOK), F32)),
         in_specs=[hbm] * 6,
-        out_specs=(hbm, hbm, hbm),
+        out_specs=(vmem, vmem, vmem),
         scratch_shapes=[
             pltpu.VMEM((4, TOK), jnp.int32),
             pltpu.VMEM((4, TOK), F32),
             pltpu.VMEM((1, TOK), jnp.int32),
-            pltpu.VMEM((BLK, HID), BF16),
-            pltpu.VMEM((4, TOK), F32),
             pltpu.VMEM((D, TOK), BF16),
             pltpu.VMEM((D, TOK), F32),
             pltpu.VMEM((NZ, PBLK, TOK), BF16),
@@ -466,7 +463,6 @@
             pltpu.VMEM((NQ, TOK, QW), BF16),
             pltpu.VMEM((NQ, NE, NJ, CAP, QW), BF16),
             pltpu.VMEM((HID, COLS), F32),
-            pltpu.VMEM((HID, COLS), BF16),
             pltpu.VMEM((QW, HPAD), F32),
             pltpu.VMEM((NQ, PBLK, HPAD), BF16),
             pltpu.VMEM((NQ, PBLK, HPAD), BF16),
@@ -480,26 +476,20 @@
             dma((NQ, 3)), dma((NQ,)),
             dma((NQ, 6)), dma((NQ,)), dma((NQ,)), dma((NQ,)),
             dma((NQ, 5)), dma((NQ,)),
-            dma((NQ, 2)), dma((NQ, 2)), dma((NQ, 2)), dma((NQ, 2)),
+            dma((NQ, CUTS)), dma((NQ, CUTS)), dma((NQ, CUTS)), dma((NQ, CUTS)),
             dma((7,)), dma((7,)), dma((3,)), dma((3,)),
-            dma((3,)),
         ],
         compiler_params=pltpu.CompilerParams(
-            collective_id=0, has_side_effects=True, vmem_limit_bytes=64 * 1024 * 1024
+            collective_id=0, has_side_effects=True, vmem_limit_bytes=60 * 1024 * 1024
         ),
     )(upstream.T, expert_ids.T, router_logits.T, guard_mask.reshape(1, TOK), w_down, saved_hidden)
     gh, gd, gl = pl.pallas_call(
         hand_over,
         out_shape=outs,
-        in_specs=[hbm] * 3,
+        in_specs=[vmem] * 3,
         out_specs=(hbm, hbm, hbm),
-        scratch_shapes=[
-            pltpu.VMEM((HID, COLS), BF16),
-            pltpu.VMEM((BLK, HID), BF16),
-            pltpu.VMEM((4, TOK), F32),
-            dma((2, 3)),
-        ],
-        compiler_params=pltpu.CompilerParams(vmem_limit_bytes=64 * 1024 * 1024),
+        scratch_shapes=[dma((3,))],
+        compiler_params=pltpu.CompilerParams(vmem_limit_bytes=8 * 1024 * 1024),
     )(*results)
     return gh, gd, gl.T
 

time: 69.7 us -> 64.8 us (0.930)
  Pallas kernels: 68.9 us -> 64.1 us
    pallas_call x2, Pallas kernels: 68.9 us -> 64.1 us  [the longest x1 63.1 us: body(): pl.pallas_call(kernel, out_shape=(pltpu.VMEM((HID, COLS), BF16), pltpu.VM...]
where the time goes in v3:
time: 64.8 us; the launch traced here: 64.7 us
  Pallas kernels  64.1 us (99%)
    pallas_call x1, Pallas kernels, body(): pl.pallas_call(kernel, out_shape=(pltpu.VMEM((HID, COLS), BF16), pltpu.VM...  63.1 us

profile of v3, /device:TPU:1, one launch (start us, length us, event | category | flops | bytes accessed | tf_op | source)
XLA Modules:
  0.0 64.7 jit_solution(12889609755617579641)
XLA Ops:
  0.6 63.1 %shard_map.85 = (bf16[360,1024]{1,0:T(8,128)(2,1)S(1)}, bf16[180,360]{1,0:T(8,128)(2,1)S(1)}, f32[4,128]{1,0:T(4,128)S(1)}) custom-call(bf16[2880,128]{1,0:T(8,128)(2,1)} %bitcast.5, s32[4,128]{1,0:T(4,128)} %bitcast.6, f32[4,128]{1,0:T(4,128)} %bitcast.7, s32[1,128]{1,0:T(1,128)} %bitcast.8, bf16[360,2880]{1,0:T(8,128)(2,1)} %w_hbm.1, bf16[360,1024]{1,0:T(8,128)(2,1)} %h_hbm.1), custom_call_target="tpu_custom_call" | custom-call | tf_op jit(solution)/shard_map/pallas_call | solution.py:445
  63.8 0.9 %shard_map.86 = (bf16[360,1024]{1,0:T(8,128)(2,1)}, bf16[180,360]{1,0:T(8,128)(2,1)}, f32[4,128]{1,0:T(4,128)}) custom-call(bf16[360,1024]{1,0:T(8,128)(2,1)S(1)} %get-tuple-element.9.gh_in, bf16[180,360]{1,0:T(8,128)(2,1)S(1)} %get-tuple-element.10.gd_in, f32[4,128]{1,0:T(4,128)S(1)} %get-tuple-element.11.gl_in), custom_call_target="tpu_custom_call" | custom-call | tf_op jit(solution)/shard_map/pallas_call | solution.py:486

commit v4 on v3

--- a/solution.py
+++ b/solution.py
@@ -224,6 +224,9 @@
     rest(2)
     cp_h.wait()
     forward(1)
+    make_rows(5)
+    start(5)
+    rest(3)
 
     def plus_send(t, k):
         at = pl.ds(k * PART, PART)
@@ -304,14 +307,14 @@
     def _(t):
         opposite(t)
 
-        @pl.when(t + 5 < NQ)
-        def _():
-            make_rows(t + 5)
-            start(t + 5)
-
-        @pl.when(t + 3 < NQ)
-        def _():
-            rest(t + 3)
+        @pl.when(t + 6 < NQ)
+        def _():
+            make_rows(t + 6)
+            start(t + 6)
+
+        @pl.when(t + 4 < NQ)
+        def _():
+            rest(t + 4)
 
         @pl.when(t > 0)
         def _():

time: 64.8 us -> 63.9 us (0.986)
  Pallas kernels: 64.1 us -> 63.2 us
    pallas_call x1, Pallas kernels: 63.1 us -> 62.2 us  [body(): pl.pallas_call(kernel, out_shape=(pltpu.VMEM((HID, COLS), BF16), pltpu.VM...]
where the time goes in v4:
time: 63.9 us; the launch traced here: 63.8 us
  Pallas kernels  63.2 us (99%)
  between operations  0.64 us (1%)
    pallas_call x1, Pallas kernels, body(): pl.pallas_call(kernel, out_shape=(pltpu.VMEM((HID, COLS), BF16), pltpu.VM...  62.2 us

profile of v4, /device:TPU:1, one launch (start us, length us, event | category | flops | bytes accessed | tf_op | source)
XLA Modules:
  0.0 63.8 jit_solution(14064749209660191263)
XLA Ops:
  0.6 62.2 %shard_map.85 = (bf16[360,1024]{1,0:T(8,128)(2,1)S(1)}, bf16[180,360]{1,0:T(8,128)(2,1)S(1)}, f32[4,128]{1,0:T(4,128)S(1)}) custom-call(bf16[2880,128]{1,0:T(8,128)(2,1)} %bitcast.5, s32[4,128]{1,0:T(4,128)} %bitcast.6, f32[4,128]{1,0:T(4,128)} %bitcast.7, s32[1,128]{1,0:T(1,128)} %bitcast.8, bf16[360,2880]{1,0:T(8,128)(2,1)} %w_hbm.1, bf16[360,1024]{1,0:T(8,128)(2,1)} %h_hbm.1), custom_call_target="tpu_custom_call" | custom-call | tf_op jit(solution)/shard_map/pallas_call | solution.py:448
  62.9 0.9 %shard_map.86 = (bf16[360,1024]{1,0:T(8,128)(2,1)}, bf16[180,360]{1,0:T(8,128)(2,1)}, f32[4,128]{1,0:T(4,128)}) custom-call(bf16[360,1024]{1,0:T(8,128)(2,1)S(1)} %get-tuple-element.9.gh_in, bf16[180,360]{1,0:T(8,128)(2,1)S(1)} %get-tuple-element.10.gd_in, f32[4,128]{1,0:T(4,128)S(1)} %get-tuple-element.11.gl_in), custom_call_target="tpu_custom_call" | custom-call | tf_op jit(solution)/shard_map/pallas_call | solution.py:489
